TPU v7x, 32 devices: a whole 2x2x4 slice. The times are simulated.
32 devices in a mesh: parts: 2 (over y), blk: 8 (over z, x), layer: 2 (over core).
Axes of the slice: x: 2, y: 2, z: 4, core: 2. Of those that a mesh axis runs over, the one named last changes fastest.
Arguments:
- query_grads: bfloat16 [2, 128, 2048], P('layer', ('parts', 'blk')), parts along dimension 1, may hold values from -0.09375 to 0.09375
- train_grads: bfloat16 [2, 12288, 2048], P('layer', ('parts', 'blk')), parts along dimension 1, may hold values from -6 to 6
- fisher: bfloat16 [2, 2048, 2048], P('layer', 'blk'), as said below
Outputs:
- scores: bfloat16 [64, 12288], P(None, ('parts', 'blk', 'layer')), parts along dimension 1
There are 2 independent parts, one for each index of `parts`. A program takes and returns all parts, laid end to end along the dimension named above; an argument that names none is the same for every part. Nothing has to cross between parts.
Inputs may be any that keep to these rules, and one draw needn't show every extreme that they name: `fisher`: each layer's block is symmetric.
All inputs are finite; a program needn't handle non-finite values.
Results may differ from a plain program's by a relative error of at most 0.005.
Values may be sent and summed in bfloat16 or wider, within the bound.
A program may use at most 64 MiB of HBM per device.

v0:
```python
import jax
import jax.numpy as jnp
from jax import lax
from jax.sharding import PartitionSpec as P


def local(query_grads, train_grads, fisher):
    queries = query_grads[0]
    training = train_grads[0]
    fisher_block = fisher[0]
    contract = (((1,), (1,)), ((), ()))
    prepared_local = jnp.dot(
        queries,
        lax.all_gather(fisher_block, "blk", axis=0, tiled=True),
        preferred_element_type=jnp.float32,
    ).astype(jnp.bfloat16)
    partial_scores = lax.dot_general(
        lax.all_gather(prepared_local, "blk", axis=0, tiled=True),
        training,
        contract,
        preferred_element_type=jnp.float32,
    )
    summed = lax.psum_scatter(partial_scores, "layer", scatter_dimension=1, tiled=True)
    return summed.astype(jnp.bfloat16)


def solution(mesh):
    return jax.shard_map(
        local,
        mesh=mesh,
        in_specs=(
            P("layer", ("parts", "blk"), None),
            P("layer", ("parts", "blk"), None),
            P("layer", "blk", None),
        ),
        out_specs=P(None, ("parts", "blk", "layer")),
        check_vma=False,
    )
```

profile of v0, /device:TPU:0, one launch (start us, length us, event | category | flops | bytes accessed | tf_op | source)
XLA Modules:
  0.0 188.5 jit_solution(18392213598629803791)
XLA Ops:
  6.5 0.0 copy-start
  6.5 0.0 all-gather.3.cloned.1.call-start
  6.5 0.7 all-gather.3.cloned.1.call-update
  7.3 0.0 reduce-scatter.2.cloned.1.call-start
  7.3 129.8 %all-gather.3.cloned.1.call-done = bf16[1,2048,2048]{2,1,0:T(8,128)(2,1)} async-done(((bf16[1,256,2048]{2,1,0:T(8,128)(2,1)}), bf16[1,2048,2048]{2,1,0:T(8,128)(2,1)}) %all-gather.3.cloned.1.call-update) | async-done | bytes 8388624 | tf_op jit(solution)/shard_map/all_gather | solution.py:14
  137.1 4.6 %fusion.4 = bf16[8,2048]{1,0:T(8,128)(2,1)S(1)} fusion(bf16[1,2048,2048]{2,1,0:T(8,128)(2,1)} %all-gather.3.cloned.1.call-done, bf16[1,8,2048]{2,1,0:T(8,128)(2,1)} %param.3), kind=kOutput, calls=%fused_computation.4 | convolution fusion | flops 67125248 | bytes 8454144 | tf_op jit(solution)/shard_map/dot_general | solution.py:12
  141.7 30.8 %all_gather.7 = bf16[64,2048]{1,0:T(8,128)(2,1)S(1)} all-gather(bf16[8,2048]{1,0:T(8,128)(2,1)S(1)} %fusion.4), channel_id=1, replica_groups=mesh['parts'=2,'blk'=8,'layer'=2] {'blk'}, dimensions={0}, use_global_device_ids=true | all-gather | bytes 294912 | tf_op jit(solution)/shard_map/all_gather | solution.py:18
  172.5 0.0 copy-done
  172.5 1.8 fusion.2
  174.3 0.0 reduce-scatter.2.cloned.1.call-update
  174.3 5.8 %reduce-scatter.2.cloned.1.call-done = f32[64,384]{1,0:T(8,128)} async-done(((f32[64,768]{1,0:T(8,128)}), f32[64,384]{1,0:T(8,128)}) %reduce-scatter.2.cloned.1.call-update) | async-done | bytes 98320 | tf_op jit(solution)/shard_map/reduce_scatter | solution.py:23
  180.1 1.5 convert_element_type.7
Async XLA Ops:
  6.5 166.0 %copy-start = (bf16[1,768,2048]{2,1,0:T(8,128)(2,1)S(1)}, bf16[1,768,2048]{2,1,0:T(8,128)(2,1)}, u32[]{:S(2)}) copy-start(bf16[1,768,2048]{2,1,0:T(8,128)(2,1)} %param.4) | copy-start | bytes 9437188
  6.5 130.6 %all-gather.3.cloned.1.call-start = ((), (), s32[]{:S(2)}) async-start(), calls=%async_computation.2 | async-start | bytes 9437184 | tf_op jit(solution)/shard_map/all_gather | solution.py:14
  7.3 172.8 %reduce-scatter.2.cloned.1.call-start = ((), (), s32[]{:S(2)}) async-start(), calls=%async_computation.1 | async-start | bytes 294912 | tf_op jit(solution)/shard_map/reduce_scatter | solution.py:23
Sparse Core Ops, SparseCore 0:
  9.5 127.6 all-gather.2
  174.4 5.6 reduce-scatter.1
where the time goes:
time: 189 us; the launch traced here: 188 us
  waiting for transfers between devices  136 us (72%)
  blocking collectives  30.8 us (16%)
  between operations  13.4 us (7%)
  matrix products  6.34 us (3%)
    all_gather x1, waiting for transfers between devices, local(): lax.all_gather(fisher_block, 'blk', axis=0, tiled=True)  130 us
    all_gather x1, blocking collectives, local(): lax.all_gather(prepared_local, 'blk', axis=0, tiled=True)  30.8 us
    reduce_scatter x1, waiting for transfers between devices, local(): lax.psum_scatter(partial_scores, 'layer', scatter_dimension=1, tiled=True)  5.82 us
    dot_general x1, matrix products, local(): jnp.dot(queries, lax.all_gather(fisher_block, 'blk', axis=0, tiled=True),...  4.59 us
  transfers between devices with their start and end apart: 2, of which 2 were waited for; matrix products, arithmetic and copies ran while one was open for 0% of the time, Pallas kernels for 0%

commit v1 on v0

v1 whole, which is shorter than its diff:
```python
import functools

import jax
import jax.numpy as jnp
from jax import lax
from jax.experimental import pallas as pl
from jax.experimental.pallas import tpu as pltpu
from jax.sharding import PartitionSpec as P

MESH = pl.DeviceIdType.MESH
CONTRACT = (((1,), (1,)), ((), ()))


def dot_t(a, b):
    return lax.dot_general(a, b, CONTRACT, preferred_element_type=jnp.float32)


def kernel(n, q_ref, t_ref, f_ref, out_ref, q_all, t_all, f_all, p_all, part, other,
           q_send, q_recv, p_send, p_recv, s_send, s_recv, in_sem):
    me = lax.axis_index("blk")
    layer = lax.axis_index("layer")
    half = t_all.shape[1]
    width = f_all.shape[0]

    load_q = pltpu.make_async_copy(q_ref.at[0], q_all.at[me], in_sem.at[0])
    load_f = pltpu.make_async_copy(f_ref.at[0], f_all, in_sem.at[1])
    load_t = [
        pltpu.make_async_copy(
            t_ref.at[0, pl.ds(pl.multiple_of(start * half, half), half), :], t_all.at[slot], in_sem.at[2 + slot]
        )
        for slot, start in ((0, 1 - layer), (1, layer))
    ]
    load_q.start()
    load_f.start()
    load_t[0].start()
    load_t[1].start()

    barrier = pltpu.get_barrier_semaphore()
    for step in range(1, n):
        pl.semaphore_signal(barrier, inc=1, device_id={"blk": lax.rem(me + step, n)}, device_id_type=MESH)
    pl.semaphore_signal(barrier, inc=1, device_id={"layer": 1 - layer}, device_id_type=MESH)
    load_q.wait()
    pl.semaphore_wait(barrier, n)

    def push(buf, step, send, recv):
        return pltpu.make_async_remote_copy(
            src_ref=buf.at[me], dst_ref=buf.at[me], send_sem=send.at[step], recv_sem=recv.at[step],
            device_id={"blk": lax.rem(me + step, n)}, device_id_type=MESH,
        )

    def arrival(buf, step, send, recv):
        source = lax.rem(me + n - step, n)
        return pltpu.make_async_remote_copy(
            src_ref=buf.at[source], dst_ref=buf.at[source], send_sem=send.at[step], recv_sem=recv.at[step],
            device_id={"blk": lax.rem(me + step, n)}, device_id_type=MESH,
        )

    for step in range(1, n):
        push(q_all, step, q_send, q_recv).start()
    load_f.wait()
    for step in range(1, n):
        arrival(q_all, step, q_send, q_recv).wait_recv()
    queries = q_all[...].reshape(-1, q_all.shape[2])
    p_all[me] = dot_t(queries, f_all[...]).astype(jnp.bfloat16)
    for step in range(1, n):
        push(p_all, step, p_send, p_recv).start()
    load_t[0].wait()
    load_t[1].wait()

    def term(source):
        columns = pl.ds(pl.multiple_of(source * width, width), width)
        block = p_all[source]
        for slot in range(2):
            yield dot_t(block, t_all[slot, :, columns])

    total = list(term(me))
    for step in range(1, n):
        arrival(p_all, step, p_send, p_recv).wait_recv()
        total = [a + b for a, b in zip(total, term(lax.rem(me + n - step, n)))]
    part[...] = total[0]
    swap = pltpu.make_async_remote_copy(
        src_ref=part, dst_ref=other, send_sem=s_send, recv_sem=s_recv,
        device_id={"layer": 1 - layer}, device_id_type=MESH,
    )
    swap.start()
    for step in range(1, n):
        push(q_all, step, q_send, q_recv).wait_send()
        push(p_all, step, p_send, p_recv).wait_send()
    swap.wait()
    out_ref[...] = (total[1] + other[...]).astype(out_ref.dtype)


def fused(n, queries, training, fisher):
    rows = queries.shape[1] * n
    k = queries.shape[2]
    half = training.shape[1] // 2
    width = fisher.shape[1]
    vmem = pltpu.VMEM
    dma = pltpu.SemaphoreType.DMA
    return pl.pallas_call(
        functools.partial(kernel, n),
        out_shape=jax.ShapeDtypeStruct((rows, half), jnp.bfloat16),
        in_specs=[pl.BlockSpec(memory_space=pltpu.HBM)] * 3,
        out_specs=pl.BlockSpec(memory_space=vmem),
        scratch_shapes=[
            vmem((n, queries.shape[1], k), jnp.bfloat16),
            vmem((2, half, k), jnp.bfloat16),
            vmem((width, k), jnp.bfloat16),
            vmem((n, rows, width), jnp.bfloat16),
            vmem((rows, half), jnp.float32),
            vmem((rows, half), jnp.float32),
            dma((n,)), dma((n,)), dma((n,)), dma((n,)), dma, dma, dma((4,)),
        ],
        compiler_params=pltpu.CompilerParams(
            collective_id=0, has_side_effects=True, vmem_limit_bytes=48 * 1024 * 1024
        ),
    )(queries, training, fisher)


def plain(queries, training, fisher):
    gathered = lax.all_gather(queries[0], "blk", axis=0, tiled=True)
    prepared_columns = dot_t(gathered, fisher[0]).astype(jnp.bfloat16)
    prepared = lax.all_gather(prepared_columns, "blk", axis=1, tiled=True)
    partial_scores = dot_t(prepared, training[0])
    summed = lax.psum_scatter(partial_scores, "layer", scatter_dimension=1, tiled=True)
    return summed.astype(jnp.bfloat16)


def solution(mesh):
    n = mesh.shape["blk"]

    def local(queries, training, fisher):
        if n > 16 or fisher.shape[1] % 128:
            return plain(queries, training, fisher)
        return fused(n, queries, training, fisher)

    return jax.shard_map(
        local,
        mesh=mesh,
        in_specs=(
            P("layer", ("parts", "blk"), None),
            P("layer", ("parts", "blk"), None),
            P("layer", "blk", None),
        ),
        out_specs=P(None, ("parts", "blk", "layer")),
        check_vma=False,
    )
```

time: 189 us -> 26.7 us (0.14)
  waiting for transfers between devices: 136 us -> 0 us
  blocking collectives: 30.8 us -> 0 us
  Pallas kernels: 0 us -> 21.9 us
  between operations: 13.4 us -> 0.01 us
  matrix products: 6.34 us -> 0 us
  local copies, waits for them, and re-layouts: 0.01 us -> 4.49 us
    all_gather x1 -> x0, waiting for transfers between devices: 130 us -> none  [local(): lax.all_gather(fisher_block, 'blk', axis=0, tiled=True)]
    all_gather x1 -> x0, blocking collectives: 30.8 us -> none  [local(): lax.all_gather(prepared_local, 'blk', axis=0, tiled=True)]
    pallas_call x0 -> x1, Pallas kernels: none -> 21.9 us  [fused(): pl.pallas_call(functools.partial(kernel, n), out_shape=jax.ShapeDtypeStru...]
    dot_general x2 -> x0, matrix products: 6.34 us -> none  [the longest x1 4.59 us: local(): jnp.dot(queries, lax.all_gather(fisher_block, 'blk', axis=0, tiled=True),...]
    reduce_scatter x1 -> x0, waiting for transfers between devices: 5.82 us -> none  [local(): lax.psum_scatter(partial_scores, 'layer', scatter_dimension=1, tiled=True)]
    unnamed x2 -> x7, local copies, waits for them, and re-layouts: 0.01 us -> 4.49 us
  transfers between devices with their start and end apart: 2 -> 0, of which waited for: 2 -> 0; matrix products, arithmetic and copies ran while one was open for 0% -> 0% of each run, Pallas kernels for 0% -> 0%
where the time goes in v1:
time: 26.7 us; the launch traced here: 26.4 us
  Pallas kernels  21.9 us (82%)
  local copies, waits for them, and re-layouts  4.49 us (17%)
    pallas_call x1, Pallas kernels, fused(): pl.pallas_call(functools.partial(kernel, n), out_shape=jax.ShapeDtypeStru...  21.9 us
    unnamed x7, local copies, waits for them, and re-layouts  4.49 us

profile of v1, /device:TPU:0, one launch (start us, length us, event | category | flops | bytes accessed | tf_op | source)
XLA Modules:
  0.0 26.4 jit_solution(18413664174898128010)
XLA Ops:
  0.0 0.0 copy-start
  0.0 1.9 %copy-done = bf16[1,768,2048]{2,1,0:T(8,128)(2,1)S(1)} copy-done((bf16[1,768,2048]{2,1,0:T(8,128)(2,1)S(1)}, bf16[1,768,2048]{2,1,0:T(8,128)(2,1)}, u32[]{:S(2)}) %copy-start) | copy-done | bytes 3145752
  1.9 0.0 copy-start.1
  1.9 1.2 %copy-done.1 = bf16[1,256,2048]{2,1,0:T(8,128)(2,1)S(1)} copy-done((bf16[1,256,2048]{2,1,0:T(8,128)(2,1)S(1)}, bf16[1,256,2048]{2,1,0:T(8,128)(2,1)}, u32[]{:S(2)}) %copy-start.1) | copy-done | bytes 1048600
  3.1 0.0 copy-start.2
  3.1 0.8 %copy-done.2 = bf16[1,8,2048]{2,1,0:T(8,128)(2,1)S(1)} copy-done((bf16[1,8,2048]{2,1,0:T(8,128)(2,1)S(1)}, bf16[1,8,2048]{2,1,0:T(8,128)(2,1)}, u32[]{:S(2)}) %copy-start.2) | copy-done | bytes 32792
  3.9 21.9 %shard_map.37 = bf16[64,384]{1,0:T(8,128)(2,1)S(1)} custom-call(bf16[1,8,2048]{2,1,0:T(8,128)(2,1)S(1)} %copy-done.2, bf16[1,768,2048]{2,1,0:T(8,128)(2,1)S(1)} %copy-done, bf16[1,256,2048]{2,1,0:T(8,128)(2,1)S(1)} %copy-done.1), custom_call_target="tpu_custom_call" | custom-call | tf_op jit(solution)/shard_map/pallas_call | solution.py:100
  25.8 0.6 %copy.5 = bf16[64,384]{1,0:T(8,128)(2,1)} copy(bf16[64,384]{1,0:T(8,128)(2,1)S(1)} %shard_map.37) | data formatting | bytes 98304
Async XLA Ops:
  0.0 1.9 %copy-start = (bf16[1,768,2048]{2,1,0:T(8,128)(2,1)S(1)}, bf16[1,768,2048]{2,1,0:T(8,128)(2,1)}, u32[]{:S(2)}) copy-start(bf16[1,768,2048]{2,1,0:T(8,128)(2,1)} %t_ref.1) | copy-start | bytes 9437188
  1.9 1.2 %copy-start.1 = (bf16[1,256,2048]{2,1,0:T(8,128)(2,1)S(1)}, bf16[1,256,2048]{2,1,0:T(8,128)(2,1)}, u32[]{:S(2)}) copy-start(bf16[1,256,2048]{2,1,0:T(8,128)(2,1)} %f_ref.1) | copy-start | bytes 3145732
  3.1 0.8 %copy-start.2 = (bf16[1,8,2048]{2,1,0:T(8,128)(2,1)S(1)}, bf16[1,8,2048]{2,1,0:T(8,128)(2,1)}, u32[]{:S(2)}) copy-start(bf16[1,8,2048]{2,1,0:T(8,128)(2,1)} %q_ref.1) | copy-start | bytes 98308

commit v2 on v1

--- a/solution.py
+++ b/solution.py
@@ -15,7 +15,7 @@
     return lax.dot_general(a, b, CONTRACT, preferred_element_type=jnp.float32)
 
 
-def kernel(n, q_ref, t_ref, f_ref, out_ref, q_all, t_all, f_all, p_all, part, other,
+def kernel(n, q_ref, t_ref, f_ref, out_ref, q_all, t_all, f_all, p_all, part, mine, other,
            q_send, q_recv, p_send, p_recv, s_send, s_recv, in_sem):
     me = lax.axis_index("blk")
     layer = lax.axis_index("layer")
@@ -35,59 +35,63 @@
     load_t[0].start()
     load_t[1].start()
 
+    targets = [lax.rem(me + i, n) for i in range(n)]
+    sources = [lax.rem(me + n - i, n) for i in range(n)]
+    cut = n // 2 - 1
+    early, late = range(n - 1, cut, -1), range(cut, 0, -1)
+
     barrier = pltpu.get_barrier_semaphore()
-    for step in range(1, n):
-        pl.semaphore_signal(barrier, inc=1, device_id={"blk": lax.rem(me + step, n)}, device_id_type=MESH)
+    for i in range(1, n):
+        pl.semaphore_signal(barrier, inc=1, device_id={"blk": targets[i]}, device_id_type=MESH)
     pl.semaphore_signal(barrier, inc=1, device_id={"layer": 1 - layer}, device_id_type=MESH)
     load_q.wait()
     pl.semaphore_wait(barrier, n)
 
-    def push(buf, step, send, recv):
+    def push(buf, at, i, send, recv):
         return pltpu.make_async_remote_copy(
-            src_ref=buf.at[me], dst_ref=buf.at[me], send_sem=send.at[step], recv_sem=recv.at[step],
-            device_id={"blk": lax.rem(me + step, n)}, device_id_type=MESH,
+            src_ref=buf.at[at], dst_ref=buf.at[at], send_sem=send.at[i], recv_sem=recv.at[i],
+            device_id={"blk": targets[i]}, device_id_type=MESH,
         )
 
-    def arrival(buf, step, send, recv):
-        source = lax.rem(me + n - step, n)
-        return pltpu.make_async_remote_copy(
-            src_ref=buf.at[source], dst_ref=buf.at[source], send_sem=send.at[step], recv_sem=recv.at[step],
-            device_id={"blk": lax.rem(me + step, n)}, device_id_type=MESH,
-        )
-
-    for step in range(1, n):
-        push(q_all, step, q_send, q_recv).start()
+    for i in range(1, n):
+        push(q_all, me, i, q_send, q_recv).start()
     load_f.wait()
-    for step in range(1, n):
-        arrival(q_all, step, q_send, q_recv).wait_recv()
+    for i in range(1, n):
+        push(q_all, sources[i], i, q_send, q_recv).wait_recv()
     queries = q_all[...].reshape(-1, q_all.shape[2])
     p_all[me] = dot_t(queries, f_all[...]).astype(jnp.bfloat16)
-    for step in range(1, n):
-        push(p_all, step, p_send, p_recv).start()
+    for i in range(1, n):
+        push(p_all, me, i, p_send, p_recv).start()
     load_t[0].wait()
     load_t[1].wait()
 
-    def term(source):
+    def term(source, slot):
         columns = pl.ds(pl.multiple_of(source * width, width), width)
-        block = p_all[source]
-        for slot in range(2):
-            yield dot_t(block, t_all[slot, :, columns])
+        return dot_t(p_all[source], t_all[slot, :, columns])
 
-    total = list(term(me))
-    for step in range(1, n):
-        arrival(p_all, step, p_send, p_recv).wait_recv()
-        total = [a + b for a, b in zip(total, term(lax.rem(me + n - step, n)))]
-    part[...] = total[0]
+    total = [term(me, 0), term(me, 1)]
+    for i in early:
+        push(p_all, sources[i], i, p_send, p_recv).wait_recv()
+        total = [total[slot] + term(sources[i], slot) for slot in range(2)]
+    mine[...] = total[1]
+    total = total[0]
+    for i in late:
+        push(p_all, sources[i], i, p_send, p_recv).wait_recv()
+        total = total + term(sources[i], 0)
+    part[...] = total
     swap = pltpu.make_async_remote_copy(
         src_ref=part, dst_ref=other, send_sem=s_send, recv_sem=s_recv,
         device_id={"layer": 1 - layer}, device_id_type=MESH,
     )
     swap.start()
-    for step in range(1, n):
-        push(q_all, step, q_send, q_recv).wait_send()
-        push(p_all, step, p_send, p_recv).wait_send()
+    total = mine[...]
+    for i in late:
+        total = total + term(sources[i], 1)
+    for i in range(1, n):
+        push(q_all, me, i, q_send, q_recv).wait_send()
+        push(p_all, me, i, p_send, p_recv).wait_send()
     swap.wait()
-    out_ref[...] = (total[1] + other[...]).astype(out_ref.dtype)
+    out_ref[...] = (total + other[...]).astype(out_ref.dtype)
 
 
 def fused(n, queries, training, fisher):
@@ -109,10 +113,11 @@
             vmem((n, rows, width), jnp.bfloat16),
             vmem((rows, half), jnp.float32),
             vmem((rows, half), jnp.float32),
+            vmem((rows, half), jnp.float32),
             dma((n,)), dma((n,)), dma((n,)), dma((n,)), dma, dma, dma((4,)),
         ],
         compiler_params=pltpu.CompilerParams(
-            collective_id=0, has_side_effects=True, vmem_limit_bytes=48 * 1024 * 1024
+            collective_id=0, has_side_effects=True, vmem_limit_bytes=63 * 1024 * 1024
         ),
     )(queries, training, fisher)
 
@@ -130,7 +135,7 @@
     n = mesh.shape["blk"]
 
     def local(queries, training, fisher):
-        if n > 16 or fisher.shape[1] % 128:
+        if n > 16 or n % 2 or fisher.shape[1] % 128:
             return plain(queries, training, fisher)
         return fused(n, queries, training, fisher)
 

time: 26.7 us -> 22.6 us (0.85)
  local copies, waits for them, and re-layouts: 4.49 us -> 1.42 us
  Pallas kernels: 21.9 us -> 20.8 us
    unnamed x7 -> x1, local copies, waits for them, and re-layouts: 4.49 us -> 1.42 us
    pallas_call x1, Pallas kernels: 21.9 us -> 20.8 us  [fused(): pl.pallas_call(functools.partial(kernel, n), out_shape=jax.ShapeDtypeStru...]
where the time goes in v2:
time: 22.6 us; the launch traced here: 22.2 us
  Pallas kernels  20.8 us (92%)
  local copies, waits for them, and re-layouts  1.42 us (6%)
    pallas_call x1, Pallas kernels, fused(): pl.pallas_call(functools.partial(kernel, n), out_shape=jax.ShapeDtypeStru...  20.8 us
    unnamed x1, local copies, waits for them, and re-layouts  1.42 us

profile of v2, /device:TPU:0, one launch (start us, length us, event | category | flops | bytes accessed | tf_op | source)
XLA Modules:
  0.0 22.2 jit_solution(1786376609584968676)
XLA Ops:
  0.0 20.8 %shard_map.37 = bf16[64,384]{1,0:T(8,128)(2,1)} custom-call(bf16[1,8,2048]{2,1,0:T(8,128)(2,1)} %q_ref.1, bf16[1,768,2048]{2,1,0:T(8,128)(2,1)} %t_ref.1, bf16[1,256,2048]{2,1,0:T(8,128)(2,1)} %f_ref.1), custom_call_target="tpu_custom_call" | custom-call | tf_op jit(solution)/shard_map/pallas_call | solution.py:104
  20.8 1.4 %copy.5 = bf16[64,384]{1,0:T(8,128)(2,1)} copy(bf16[64,384]{1,0:T(8,128)(2,1)} %shard_map.37) | data formatting | bytes 98304

commit v3 on v2

--- a/solution.py
+++ b/solution.py
@@ -53,7 +53,7 @@
             device_id={"blk": targets[i]}, device_id_type=MESH,
         )
 
-    for i in range(1, n):
+    for i in [*range(n - 1, 0, -2), *range(n - 2, 0, -2)]:
         push(q_all, me, i, q_send, q_recv).start()
     load_f.wait()
     for i in range(1, n):

time: 22.6 us -> 22.2 us (0.982)
  the two profiles are of different devices: /device:TPU:0 before, /device:TPU:11 now
where the time goes in v3:
time: 22.2 us; the launch traced here: 22 us
  Pallas kernels  20.6 us (93%)
  local copies, waits for them, and re-layouts  1.42 us (6%)
    pallas_call x1, Pallas kernels, fused(): pl.pallas_call(functools.partial(kernel, n), out_shape=jax.ShapeDtypeStru...  20.6 us
    unnamed x1, local copies, waits for them, and re-layouts  1.42 us

profile of v3, /device:TPU:11, one launch (start us, length us, event | category | flops | bytes accessed | tf_op | source)
XLA Modules:
  0.0 22.0 jit_solution(15384582365065013378)
XLA Ops:
  0.0 20.6 %shard_map.37 = bf16[64,384]{1,0:T(8,128)(2,1)} custom-call(bf16[1,8,2048]{2,1,0:T(8,128)(2,1)} %q_ref.1, bf16[1,768,2048]{2,1,0:T(8,128)(2,1)} %t_ref.1, bf16[1,256,2048]{2,1,0:T(8,128)(2,1)} %f_ref.1), custom_call_target="tpu_custom_call" | custom-call | tf_op jit(solution)/shard_map/pallas_call | solution.py:104
  20.6 1.4 %copy.5 = bf16[64,384]{1,0:T(8,128)(2,1)} copy(bf16[64,384]{1,0:T(8,128)(2,1)} %shard_map.37) | data formatting | bytes 98304
